TPU v7x, 32 devices: a whole 2x2x4 slice. The times are simulated.
32 devices in a mesh: sub: 16 (over z, y, x), rhs: 2 (over core).
Axes of the slice: x: 2, y: 2, z: 4, core: 2. Of those that a mesh axis runs over, the one named last changes fastest.
Arguments:
- schur_block: bfloat16 [32, 1024, 1024], P('sub', 'rhs'), may hold values from -1 to 4, as said below
- scaling: float32 [32, 1024], P('sub'), may hold values from 0.25 to 1.75
- gravity_load: float32 [32, 1024, 256], P('sub', None, 'rhs'), may hold values from -100 to 100
- pressure: bfloat16 [1024, 4, 256], P('sub', None, 'rhs'), may hold values from -6 to 6
- block_target: int32 [1024, 1], P('sub'), may hold values from 0 to 31; in each aligned block of 64 rows (0 to 63, 64 to 127, ...) at most 4 rows name the same one
- aero_interp: float32 [4, 1024], replicated, may hold values from -0.5 to 0.5
- partner_slot: int32 [4, 32], P(None, 'sub'), may hold values from 0 to 1, as said below
- corner_row: int32 [32, 8], P('sub'), may hold values from 0 to 1023
- corner_coarse: int32 [32, 8], P('sub'), may hold values from 0 to 127
- coarse_inverse: float32 [128, 128], P('sub'), may hold values from -1 to 6, as said below
Outputs:
- solution: float32 [32, 1024, 256], P('sub', None, 'rhs')
Inputs may be any that keep to these rules, and one draw needn't show every extreme that they name: `block_target`: at most 4 of the blocks of one device name the same subdomain; in some device's blocks one subdomain is named exactly 4 times; every subdomain is named by some block. In round k, subdomain s on device d = s // 2 is paired with subdomain (d xor 2^k) * 2 + partner_slot[k, s]; the pairing is mutual. `schur_block`: each matrix is symmetric. `coarse_inverse`: symmetric.
All inputs are finite; a program needn't handle non-finite values.
Results may differ from a plain program's by a relative error of at most 0.0027.
Values may be sent and summed in bfloat16 or wider, within the bound.
A program may use at most 64 MiB of HBM per device.

v0:
```python
import jax
import jax.numpy as jnp
from jax import lax
from jax.sharding import PartitionSpec as P

SUB_DEV = 2
FACES = 4
MOST = 4
ITERS = 2
FW = 256
coupling = 2.0


def swapped(shard, axis, distance):
    return lax.ppermute(shard, axis, [(i, i ^ 1 << distance) for i in range(lax.axis_size(axis))])


def schur_apply(schur_block, rounded):
    half_rows = jnp.einsum(
        "snm,smc->snc",
        schur_block,
        lax.all_gather(rounded, "rhs", axis=2, tiled=True),
        preferred_element_type=jnp.float32,
    )
    return lax.all_to_all(half_rows, "rhs", split_axis=2, concat_axis=1, tiled=True)


def jump_terms(rounded, partner_slot):
    face_terms = []
    for face_index in range(FACES):
        own_face = rounded[:, face_index * FW : (face_index + 1) * FW, :]
        partner_face = swapped(own_face, "sub", face_index)
        select = (
            partner_slot[face_index][:, None] == jnp.arange(SUB_DEV, dtype=jnp.int32)[None, :]
        ).astype(jnp.bfloat16)
        picked = jnp.einsum("sj,jfc->sfc", select, partner_face, preferred_element_type=jnp.float32)
        face_terms.append(coupling * (own_face.astype(jnp.float32) - picked))
    return jnp.concatenate(face_terms, axis=1)


def operator(direction, schur_block, partner_slot):
    rounded = direction.astype(jnp.bfloat16)
    return schur_apply(schur_block, rounded) + jump_terms(rounded, partner_slot)


def coarse_solve(coarse, coarse_inverse):
    own_rows = jnp.dot(coarse_inverse, coarse, precision=lax.Precision.HIGHEST)
    return lax.all_gather(own_rows, "sub", axis=0, tiled=True)


def add_corners(solved, corner_row, corner_coarse, residual):
    sub_rows = jnp.arange(SUB_DEV, dtype=jnp.int32)[:, None]
    return jnp.zeros_like(residual).at[sub_rows, corner_row].add(solved[corner_coarse])


def precondition(residual, schur_block, scaling, corner_row, corner_coarse, coarse_inverse):
    columns = residual.shape[2]
    weight_col = scaling[:, :, None]
    dirichlet = weight_col * schur_apply(schur_block, (weight_col * residual).astype(jnp.bfloat16))
    sub_rows = jnp.arange(SUB_DEV, dtype=jnp.int32)[:, None]
    picked = residual[sub_rows, corner_row]
    partial_sum = (
        jnp.zeros((coarse_inverse.shape[1], columns), jnp.float32)
        .at[corner_coarse.reshape(-1)]
        .add(picked.reshape(-1, columns))
    )
    coarse = lax.psum(partial_sum, "sub")
    solved = coarse_solve(coarse, coarse_inverse)
    precond = dirichlet + add_corners(solved, corner_row, corner_coarse, residual)
    product_value = lax.psum(jnp.sum(residual * precond, axis=(0, 1)), "sub")
    return (precond, product_value)


def on_device(
    schur_block,
    scaling,
    gravity_load,
    pressure,
    block_target,
    aero_interp,
    partner_slot,
    corner_row,
    corner_coarse,
    coarse_inverse,
):
    sub_count = lax.axis_size("sub")
    all_subdomains = SUB_DEV * sub_count
    columns = gravity_load.shape[2]
    points = pressure.shape[1]
    target = block_target[:, 0]
    matches = target[:, None] == target[None, :]
    before = jnp.tril(matches, -1)
    rank_in = jnp.sum(before, axis=1, dtype=jnp.int32)
    slot_index = target * MOST + rank_in
    buffer = (
        jnp.zeros((all_subdomains * MOST, points, columns), jnp.bfloat16)
        .at[slot_index]
        .set(pressure)
    )
    arrived = lax.all_to_all(buffer, "sub", split_axis=0, concat_axis=0, tiled=True)
    load_sum = jnp.sum(
        arrived.reshape(sub_count, SUB_DEV, MOST, points, columns), axis=(0, 2), dtype=jnp.float32
    )
    force_total = gravity_load + jnp.einsum(
        "pm,spc->smc", aero_interp, load_sum, precision=lax.Precision.HIGHEST
    )
    solution = jnp.zeros_like(force_total)
    residual = force_total
    precond, precond_dot = precondition(
        residual, schur_block, scaling, corner_row, corner_coarse, coarse_inverse
    )
    direction = precond
    for step_index in range(ITERS):
        applied = operator(direction, schur_block, partner_slot)
        curvature = lax.psum(jnp.sum(direction * applied, axis=(0, 1)), "sub")
        step_size = precond_dot / curvature
        solution = solution + step_size * direction
        residual = residual - step_size * applied
        if step_index + 1 < ITERS:
            precond, next_product = precondition(
                residual, schur_block, scaling, corner_row, corner_coarse, coarse_inverse
            )
            direction = precond + next_product / precond_dot * direction
            precond_dot = next_product
    return solution


def solution(mesh):
    return jax.shard_map(
        on_device,
        mesh=mesh,
        in_specs=(
            P("sub", "rhs", None),
            P("sub", None),
            P("sub", None, "rhs"),
            P("sub", None, "rhs"),
            P("sub", None),
            P(),
            P(None, "sub"),
            P("sub", None),
            P("sub", None),
            P("sub", None),
        ),
        out_specs=P("sub", None, "rhs"),
        check_vma=False,
    )
```

profile of v0, /device:TPU:0, one launch (start us, length us, event | category | flops | bytes accessed | tf_op | source)
XLA Modules:
  0.0 575.2 jit_solution(14376807275874382460)
XLA Ops:
  9.7 7.6 %scatter_fusion = bf16[128,4,128]{2,1,0:T(4,128)(2,1)} fusion(bf16[128,4,128]{2,1,0:T(4,128)(2,1)} %broadcast_in_dim.12, s32[64]{0:T(128)S(1)} %fusion.22, bf16[64,4,128]{2,1,0:T(4,128)(2,1)} %param.13), kind=kCustom, calls=%fused_computation.4 | custom fusion | bytes 196864 | tf_op jit(solution)/shard_map/scatter | solution.py:98
  17.3 8.3 %all-to-all-start = ((bf16[128,4,128]{2,1,0:T(4,128)(2,1)}), bf16[128,4,128]{2,1,0:T(4,128)(2,1)S(1)}, u32[]{:S(2)}, u32[]{:S(2)}) async-start(bf16[128,4,128]{2,1,0:T(4,128)(2,1)} %scatter_fusion), calls=%async_computation | async-start | bytes 262144 | tf_op jit(solution)/shard_map/all_to_all | solution.py:100
  27.2 2.5 copy.107
  29.7 3.7 all-to-all-done
  33.5 3.1 multiply_convert_fusion.1
  37.9 2.1 scatter_custom_fusion.1
  40.8 98.9 %all-reduce.4.cloned.1.call-done = f32[128,128]{1,0:T(8,128)} async-done(((f32[128,128]{1,0:T(8,128)}), f32[128,128]{1,0:T(8,128)}) %all-reduce.4.cloned.1.call-update) | async-done | bytes 65552 | tf_op jit(solution)/shard_map/psum | solution.py:67
  140.7 39.1 %all_gather.19 = f32[128,128]{1,0:T(8,128)S(1)} all-gather(f32[8,128]{1,0:T(8,128)S(1)} %convolution_bitcast_fusion.6), channel_id=1, replica_groups=mesh['sub'=16,'rhs'=2] {'sub'}, dimensions={0}, use_global_device_ids=true | all-gather | bytes 69632 | tf_op jit(solution)/shard_map/all_gather | solution.py:48
  180.4 2.0 convolution_bitcast_fusion.3
  183.2 4.6 all_to_all.77
  187.8 1.8 copy.151
  189.6 2.1 all_to_all.59
  192.8 2.6 copy.111
  195.4 2.2 scatter_fusion.1
  200.1 1.9 fusion.34
  204.5 3.0 collective-permute-done
  220.9 2.3 subtract_multiply_fusion.7
  223.2 2.0 convolution_bitcast_fusion.2
  226.0 4.6 all_to_all.78
  230.6 1.8 copy.150
  232.4 3.2 all_to_all.63
  235.5 2.0 multiply_reduce_fusion.1
  237.6 39.5 %all-reduce = (f32[128]{0:T(128)S(1)}, f32[128]{0:T(128)S(1)}) all-reduce(f32[128]{0:T(128)S(1)} %get-tuple-element.6, f32[128]{0:T(128)S(1)} %get-tuple-element.5), channel_id=1, replica_groups=mesh['sub'=16,'rhs'=2] {'sub'}, use_global_device_ids=true, to_apply=%region_7.8 | all-reduce | flops 256 | bytes 2048 | tf_op jit(solution)/shard_map/psum | solution.py:70
  277.1 3.3 multiply_convert_fusion
  280.3 2.5 copy.128
  282.9 2.1 scatter_custom_fusion.3
  285.6 97.4 %all-reduce.6.cloned.1.call-done = f32[128,128]{1,0:T(8,128)} async-done(((f32[128,128]{1,0:T(8,128)}), f32[128,128]{1,0:T(8,128)}) %all-reduce.6.cloned.1.call-update) | async-done | bytes 65552 | tf_op jit(solution)/shard_map/psum | solution.py:67
  384.0 39.1 %all_gather.22 = f32[128,128]{1,0:T(8,128)S(1)} all-gather(f32[8,128]{1,0:T(8,128)S(1)} %convolution_bitcast_fusion.5), channel_id=1, replica_groups=mesh['sub'=16,'rhs'=2] {'sub'}, dimensions={0}, use_global_device_ids=true | all-gather | bytes 69632 | tf_op jit(solution)/shard_map/all_gather | solution.py:48
  423.9 2.0 convolution_bitcast_fusion.1
  426.6 4.6 all_to_all.79
  431.2 1.8 copy.149
  433.0 3.1 all_to_all.67
  436.1 2.4 broadcast_multiply_fusion
  438.5 2.6 copy.129
  441.1 2.2 scatter_fusion.2
  443.3 2.5 copy.130
  447.6 36.9 %psum.46 = f32[128]{0:T(128)S(1)} all-reduce(f32[128]{0:T(128)S(1)} %multiply_reduce_fusion), channel_id=1, replica_groups=mesh['sub'=16,'rhs'=2] {'sub'}, use_global_device_ids=true, to_apply=%region_14.15 | all-reduce | flops 128 | bytes 1024 | tf_op jit(solution)/shard_map/psum | solution.py:70
  484.5 2.2 fusion.32
  486.6 1.9 fusion.33
  488.5 2.0 collective-permute-start.4
  507.3 2.3 subtract_multiply_fusion.3
  509.7 2.0 convolution_bitcast_fusion
  512.5 4.6 all_to_all.80
  518.8 3.2 all_to_all.71
  522.0 2.1 fusion.2
  524.1 38.5 %psum.47 = f32[128]{0:T(128)S(1)} all-reduce(f32[128]{0:T(128)S(1)} %fusion.2), channel_id=1, replica_groups=mesh['sub'=16,'rhs'=2] {'sub'}, use_global_device_ids=true, to_apply=%region_16.17 | all-reduce | flops 128 | bytes 1024 | tf_op jit(solution)/shard_map/psum | solution.py:115
  562.6 2.5 multiply_add_fusion
  565.1 2.5 copy.143
  (119 shorter events, 53.0 us)
Async XLA Ops:
  7.4 173.0 %copy-start = (bf16[2,512,1024]{2,1,0:T(8,128)(2,1)S(1)}, bf16[2,512,1024]{2,1,0:T(8,128)(2,1)}, u32[]{:S(2)}) copy-start(bf16[2,512,1024]{2,1,0:T(8,128)(2,1)} %param.10) | copy-start | bytes 6291460
  7.4 26.1 %copy-start.2 = (f32[2,1024]{1,0:T(2,128)S(1)}, f32[2,1024]{1,0:T(2,128)}, u32[]{:S(2)}) copy-start(f32[2,1024]{1,0:T(2,128)} %param.11) | copy-start | bytes 24580
  7.4 26.1 %copy-start.5 = (f32[4,1024]{1,0:T(4,128)S(1)}, f32[4,1024]{1,0:T(4,128)}, u32[]{:S(2)}) copy-start(f32[4,1024]{1,0:T(4,128)} %param.15) | copy-start | bytes 49156
  17.3 16.1 %all-to-all-start = ((bf16[128,4,128]{2,1,0:T(4,128)(2,1)}), bf16[128,4,128]{2,1,0:T(4,128)(2,1)S(1)}, u32[]{:S(2)}, u32[]{:S(2)}) async-start(bf16[128,4,128]{2,1,0:T(4,128)(2,1)} %scatter_fusion), calls=%async_computation | async-start | bytes 262144 | tf_op jit(solution)/shard_map/all_to_all | solution.py:100
  25.6 114.1 %all-reduce.4.cloned.1.call-start = ((), (), s32[]{:S(2)}) async-start(), calls=%async_computation.6 | async-start | bytes 131072 | tf_op jit(solution)/shard_map/psum | solution.py:67
  27.2 10.7 %copy-start.13 = (s32[16]{0:T(128)}, s32[16]{0:T(128)S(1)}, u32[]{:S(2)}) copy-start(s32[16]{0:T(128)S(1)} %reshape.57) | copy-start | bytes 196
  29.7 8.2 %copy-start.14 = (s32[16]{0:T(128)}, s32[16]{0:T(128)S(1)}, u32[]{:S(2)}) copy-start(s32[16]{0:T(128)S(1)} %fusion.23) | copy-start | bytes 196
  33.5 7.1 %copy-start.9 = (s32[2,8]{1,0:T(2,128)S(1)}, s32[2,8]{1,0:T(2,128)}, u32[]{:S(2)}) copy-start(s32[2,8]{1,0:T(2,128)} %param.18) | copy-start | bytes 196
  33.5 106.2 %copy-start.3 = (f32[8,128]{1,0:T(8,128)S(1)}, f32[8,128]{1,0:T(8,128)}, u32[]{:S(2)}) copy-start(f32[8,128]{1,0:T(8,128)} %param.19) | copy-start | bytes 12292
  36.6 145.8 %copy-start.1 = (f32[2,1024,128]{1,2,0:T(8,128)}, f32[2,1024,128]{1,2,0:T(8,128)S(1)}, u32[]{:S(2)}) copy-start(f32[2,1024,128]{1,2,0:T(8,128)S(1)} %get-tuple-element.34) | copy-start | bytes 3145732
  40.0 140.4 %all-gather.5.cloned.1.call-start = ((), (), s32[]{:S(2)}) async-start(), calls=%async_computation.5 | async-start | bytes 1572864 | tf_op jit(solution)/shard_map/all_gather | solution.py:22
  40.6 182.6 %all-gather.7.cloned.1.call-start = ((), (), s32[]{:S(2)}) async-start(), calls=%async_computation.7 | async-start | bytes 1572864 | tf_op jit(solution)/shard_map/all_gather | solution.py:22
  40.8 141.6 %copy-start.6 = (s32[1024]{0:T(1024)}, s32[1024]{0:T(1024)S(1)}, u32[]{:S(2)}) copy-start(s32[1024]{0:T(1024)S(1)} %pad_clamp_fusion) | copy-start | bytes 12292
  197.6 4.3 copy-start.4
  201.9 5.5 collective-permute-start
  202.8 180.3 %all-reduce.6.cloned.1.call-start = ((), (), s32[]{:S(2)}) async-start(), calls=%async_computation.9 | async-start | bytes 131072 | tf_op jit(solution)/shard_map/psum | solution.py:67
  203.0 7.3 %collective-permute-start.3 = (bf16[2,256,128]{1,2,0:T(8,128)(2,1)}, bf16[2,256,128]{1,2,0:T(8,128)(2,1)}, u32[]{:S(2)}, u32[]{:S(2)}) collective-permute-start(bf16[2,256,128]{1,2,0:T(8,128)(2,1)} %get-tuple-element.28), channel_id=1, source_target_pairs={{0,16},{2,18},{4,20},{6,22},{8,24},{10,26},{12,28},{14,30},{16,0},... | collective-permute-start | bytes 393224 | tf_op jit(solution)/shard_map/ppermute | solution.py:15
  203.1 11.1 %collective-permute-start.2 = (bf16[2,256,128]{1,2,0:T(8,128)(2,1)}, bf16[2,256,128]{1,2,0:T(8,128)(2,1)}, u32[]{:S(2)}, u32[]{:S(2)}) collective-permute-start(bf16[2,256,128]{1,2,0:T(8,128)(2,1)} %get-tuple-element.29), channel_id=1, source_target_pairs={{0,8},{2,10},{4,12},{6,14},{8,0},{10,2},{12,4},{14,6},{16,24},{18,... | collective-permute-start | bytes 393224 | tf_op jit(solution)/shard_map/ppermute | solution.py:15
  203.2 14.8 %collective-permute-start.1 = (bf16[2,256,128]{1,2,0:T(8,128)(2,1)}, bf16[2,256,128]{1,2,0:T(8,128)(2,1)S(1)}, u32[]{:S(2)}, u32[]{:S(2)}) collective-permute-start(bf16[2,256,128]{1,2,0:T(8,128)(2,1)} %get-tuple-element.30), channel_id=1, source_target_pairs={{0,4},{2,6},{4,0},{6,2},{8,12},{10,14},{12,8},{14,10},{16,20},{18,... | collective-permute-start | bytes 393224 | tf_op jit(solution)/shard_map/ppermute | solution.py:15
  277.1 3.3 copy-start.7
  285.0 138.8 %all-gather.9.cloned.1.call-start = ((), (), s32[]{:S(2)}) async-start(), calls=%async_computation.8 | async-start | bytes 1572864 | tf_op jit(solution)/shard_map/all_gather | solution.py:22
  285.6 224.1 %all-gather.11.cloned.1.call-start = ((), (), s32[]{:S(2)}) async-start(), calls=%async_computation.10 | async-start | bytes 1572864 | tf_op jit(solution)/shard_map/all_gather | solution.py:22
  484.4 4.0 copy-start.15
  486.6 11.9 %copy-start.12 = (s32[2]{0:T(128)S(1)}, s32[2]{0:T(128)}, u32[]{:S(2)}) copy-start(s32[2]{0:T(128)} %get-tuple-element.9) | copy-start | bytes 28
  486.6 15.7 %copy-start.11 = (s32[2]{0:T(128)S(1)}, s32[2]{0:T(128)}, u32[]{:S(2)}) copy-start(s32[2]{0:T(128)} %get-tuple-element.10) | copy-start | bytes 28
  488.5 5.0 collective-permute-start.4
  490.5 6.4 %collective-permute-start.7 = (bf16[2,256,128]{1,2,0:T(8,128)(2,1)}, bf16[2,256,128]{1,2,0:T(8,128)(2,1)}, u32[]{:S(2)}, u32[]{:S(2)}) collective-permute-start(bf16[2,256,128]{1,2,0:T(8,128)(2,1)} %get-tuple-element.20), channel_id=1, source_target_pairs={{0,16},{2,18},{4,20},{6,22},{8,24},{10,26},{12,28},{14,30},{16,0},... | collective-permute-start | bytes 393224 | tf_op jit(solution)/shard_map/ppermute | solution.py:15
  490.6 10.1 %collective-permute-start.6 = (bf16[2,256,128]{1,2,0:T(8,128)(2,1)}, bf16[2,256,128]{1,2,0:T(8,128)(2,1)}, u32[]{:S(2)}, u32[]{:S(2)}) collective-permute-start(bf16[2,256,128]{1,2,0:T(8,128)(2,1)} %get-tuple-element.21), channel_id=1, source_target_pairs={{0,8},{2,10},{4,12},{6,14},{8,0},{10,2},{12,4},{14,6},{16,24},{18,... | collective-permute-start | bytes 393224 | tf_op jit(solution)/shard_map/ppermute | solution.py:15
  490.7 14.5 %copy-start.10 = (s32[2]{0:T(128)S(1)}, s32[2]{0:T(128)}, u32[]{:S(2)}) copy-start(s32[2]{0:T(128)} %get-tuple-element.8) | copy-start | bytes 28
  490.7 13.7 %collective-permute-start.5 = (bf16[2,256,128]{1,2,0:T(8,128)(2,1)}, bf16[2,256,128]{1,2,0:T(8,128)(2,1)S(1)}, u32[]{:S(2)}, u32[]{:S(2)}) collective-permute-start(bf16[2,256,128]{1,2,0:T(8,128)(2,1)} %get-tuple-element.22), channel_id=1, source_target_pairs={{0,4},{2,6},{4,0},{6,2},{8,12},{10,14},{12,8},{14,10},{16,20},{18,... | collective-permute-start | bytes 393224 | tf_op jit(solution)/shard_map/ppermute | solution.py:15
  522.0 40.6 %copy-start.16 = (f32[128]{0:T(128)S(1)}, f32[128]{0:T(128)}, u32[]{:S(2)}) copy-start(f32[128]{0:T(128)} %copy-done.15) | copy-start | bytes 1540
  522.0 40.6 %copy-start.8 = (f32[128]{0:T(128)S(1)}, f32[128]{0:T(128)}, u32[]{:S(2)}) copy-start(f32[128]{0:T(128)} %copy-done.7) | copy-start | bytes 1540
Sparse Core Ops, SparseCore 0:
  40.1 99.5 all-reduce.3
  285.1 97.8 all-reduce.5
Sparse Core Ops, SparseCore 1:
  42.0 6.5 all-gather.4
  202.9 6.7 all-gather.6
  287.1 4.7 all-gather.8
  490.6 5.2 all-gather.10
where the time goes:
time: 577 us; the launch traced here: 575 us
  blocking collectives  211 us (37%)
  waiting for transfers between devices  206 us (36%)
  local copies, waits for them, and re-layouts  71.9 us (12%)
  other arithmetic  33.9 us (6%)
  matrix products  23 us (4%)
  between operations  15.4 us (3%)
  starting transfers between devices  13.9 us (2%)
    psum x2, waiting for transfers between devices, precondition(): coarse = lax.psum(partial_sum, 'sub')  196 us
    all_gather x2, blocking collectives, coarse_solve(): return lax.all_gather(own_rows, 'sub', axis=0, tiled=True)  78.2 us
    psum x2, blocking collectives, precondition(): product_value = lax.psum(jnp.sum(residual * precond, axis=(0, 1)), 'sub')  76.4 us
    psum x1, blocking collectives, on_device(): curvature = lax.psum(jnp.sum(direction * applied, axis=(0, 1)), 'sub')  38.5 us
    all_to_all x8, local copies, waits for them, and re-layouts, schur_apply(): lax.all_to_all(half_rows, 'rhs', split_axis=2, concat_axis=1, tiled=True)  18.7 us
    all_to_all x4, blocking collectives, schur_apply(): lax.all_to_all(half_rows, 'rhs', split_axis=2, concat_axis=1, tiled=True)  18.3 us
  transfers between devices with their start and end apart: 15, of which 6 were waited for; matrix products, arithmetic and copies ran while one was open for 7% of the time, Pallas kernels for 0%

commit v1 on v0

--- a/solution.py
+++ b/solution.py
@@ -45,7 +45,32 @@
 
 def coarse_solve(coarse, coarse_inverse):
     own_rows = jnp.dot(coarse_inverse, coarse, precision=lax.Precision.HIGHEST)
-    return lax.all_gather(own_rows, "sub", axis=0, tiled=True)
+
+    def lay_the_slices(x0, dev_axis):
+        a_next = lax.axis_size(dev_axis)
+        b_now = lax.axis_index(dev_axis)
+        x_now, y, known = (a_next, b_now, x0.shape[0])
+        row_list = [src_i * x_now if pp == 0 else src_i for pp, src_i in enumerate(x0.shape)]
+        base_arr = jnp.zeros(row_list, x0.dtype)
+        piece_next = lax.dynamic_update_slice_in_dim(base_arr, x0, y * known, axis=0)
+        f_now = latest = x0
+        for i0 in tuple(range(1, x_now // 2 + 1)):
+            f_now = lax.ppermute(
+                f_now, axis_name=dev_axis, perm=[(pp, (pp + 1) % x_now) for pp in range(x_now)]
+            )
+            piece_next = lax.dynamic_update_slice_in_dim(
+                piece_next, f_now, (y - i0) % x_now * known, axis=0
+            )
+            if 2 * i0 < x_now:
+                latest = lax.ppermute(
+                    latest, axis_name=dev_axis, perm=[(pp, (pp - 1) % x_now) for pp in range(x_now)]
+                )
+                piece_next = lax.dynamic_update_slice_in_dim(
+                    piece_next, latest, (y + i0) % x_now * known, axis=0
+                )
+        return piece_next
+
+    return lay_the_slices(own_rows, "sub")
 
 
 def add_corners(solved, corner_row, corner_coarse, residual):

time: 577 us -> 612 us (1.061)
  starting transfers between devices: 13.9 us -> 93.5 us
  blocking collectives: 211 us -> 133 us
  waiting for transfers between devices: 206 us -> 241 us
    ppermute x0 -> x30, starting transfers between devices: none -> 79.5 us  [the longest x14 76.6 us: lay_the_slices(): lax.ppermute(latest, axis_name=dev_axis, perm=[(pp, (pp - 1) % x_now) for...]
    all_gather x2 -> x0, blocking collectives: 78.2 us -> none  [coarse_solve(): return lax.all_gather(own_rows, 'sub', axis=0, tiled=True)]
    ppermute x0 -> x30, waiting for transfers between devices: none -> 35.4 us  [the longest x16 35.4 us: lay_the_slices(): lax.ppermute(f_now, axis_name=dev_axis, perm=[(pp, (pp + 1) % x_now) for...]
  transfers between devices with their start and end apart: 15 -> 45, of which waited for: 6 -> 21; matrix products, arithmetic and copies ran while one was open for 7% -> 6% of each run, Pallas kernels for 0% -> 0%
where the time goes in v1:
time: 612 us; the launch traced here: 610 us
  waiting for transfers between devices  241 us (39%)
  blocking collectives  133 us (22%)
  starting transfers between devices  93.5 us (15%)
  local copies, waits for them, and re-layouts  68.4 us (11%)
  other arithmetic  34.9 us (6%)
  matrix products  23 us (4%)
  between operations  15.5 us (3%)
    psum x2, waiting for transfers between devices, precondition(): coarse = lax.psum(partial_sum, 'sub')  198 us
    ppermute x14, starting transfers between devices, lay_the_slices(): lax.ppermute(latest, axis_name=dev_axis, perm=[(pp, (pp - 1) % x_now) for...  76.6 us
    psum x2, blocking collectives, precondition(): product_value = lax.psum(jnp.sum(residual * precond, axis=(0, 1)), 'sub')  76 us
    psum x1, blocking collectives, on_device(): curvature = lax.psum(jnp.sum(direction * applied, axis=(0, 1)), 'sub')  39 us
    ppermute x16, waiting for transfers between devices, lay_the_slices(): lax.ppermute(f_now, axis_name=dev_axis, perm=[(pp, (pp + 1) % x_now) for...  35.4 us
    all_to_all x4, blocking collectives, schur_apply(): lax.all_to_all(half_rows, 'rhs', split_axis=2, concat_axis=1, tiled=True)  18.3 us
    all_to_all x8, local copies, waits for them, and re-layouts, schur_apply(): lax.all_to_all(half_rows, 'rhs', split_axis=2, concat_axis=1, tiled=True)  17.3 us
  transfers between devices with their start and end apart: 45, of which 21 were waited for; matrix products, arithmetic and copies ran while one was open for 6% of the time, Pallas kernels for 0%

profile of v1, /device:TPU:0, one launch (start us, length us, event | category | flops | bytes accessed | tf_op | source)
XLA Modules:
  0.0 609.7 jit_solution(1924146612380288647)
XLA Ops:
  9.7 6.8 %scatter_fusion = bf16[128,4,128]{2,1,0:T(4,128)(2,1)} fusion(bf16[128,4,128]{2,1,0:T(4,128)(2,1)} %broadcast_in_dim.12, s32[64]{0:T(128)S(1)} %fusion.22, bf16[64,4,128]{2,1,0:T(4,128)(2,1)} %param.13), kind=kCustom, calls=%fused_computation.4 | custom fusion | bytes 196864 | tf_op jit(solution)/shard_map/scatter | solution.py:123
  16.6 8.3 %all-to-all-start = ((bf16[128,4,128]{2,1,0:T(4,128)(2,1)}), bf16[128,4,128]{2,1,0:T(4,128)(2,1)S(1)}, u32[]{:S(2)}, u32[]{:S(2)}) async-start(bf16[128,4,128]{2,1,0:T(4,128)(2,1)} %scatter_fusion), calls=%async_computation | async-start | bytes 262144 | tf_op jit(solution)/shard_map/all_to_all | solution.py:125
  27.1 2.5 copy.107
  29.8 2.9 all-to-all-done
  32.8 3.1 multiply_convert_fusion.1
  39.4 100.4 %all-reduce.4.cloned.1.call-done = f32[128,128]{1,0:T(8,128)} async-done(((f32[128,128]{1,0:T(8,128)}), f32[128,128]{1,0:T(8,128)}) %all-reduce.4.cloned.1.call-update) | async-done | bytes 65552 | tf_op jit(solution)/shard_map/psum | solution.py:92
  142.3 4.2 collective-permute-start.1
  148.0 5.6 collective-permute-start.3
  155.2 5.6 collective-permute-start.5
  162.4 5.6 collective-permute-start.7
  169.6 5.6 collective-permute-start.9
  176.8 5.6 collective-permute-start.11
  184.0 5.6 collective-permute-start.13
  191.2 7.2 %collective-permute-done.14 = f32[8,128]{1,0:T(8,128)S(1)} collective-permute-done((f32[8,128]{1,0:T(8,128)S(1)}, f32[8,128]{1,0:T(8,128)S(1)}, u32[]{:S(2)}, u32[]{:S(2)}) %collective-permute-start.14) | collective-permute-done | bytes 4128 | tf_op jit(solution)/shard_map/ppermute | solution.py:58
  201.9 4.6 all_to_all.77
  211.8 2.3 scatter_fusion.1
  220.9 3.0 collective-permute-done.15
  237.2 2.4 subtract_multiply_fusion.7
  242.4 4.6 all_to_all.78
  248.8 3.1 all_to_all.63
  253.9 39.5 %all-reduce = (f32[128]{0:T(128)S(1)}, f32[128]{0:T(128)S(1)}) all-reduce(f32[128]{0:T(128)S(1)} %get-tuple-element.6, f32[128]{0:T(128)S(1)} %get-tuple-element.5), channel_id=1, replica_groups=mesh['sub'=16,'rhs'=2] {'sub'}, use_global_device_ids=true, to_apply=%region_7.8 | all-reduce | flops 256 | bytes 2048 | tf_op jit(solution)/shard_map/psum | solution.py:95
  293.4 3.3 multiply_convert_fusion
  296.7 2.6 copy.128
  299.2 2.1 scatter_custom_fusion.3
  301.4 97.9 %all-reduce.6.cloned.1.call-done = f32[128,128]{1,0:T(8,128)} async-done(((f32[128,128]{1,0:T(8,128)}), f32[128,128]{1,0:T(8,128)}) %all-reduce.6.cloned.1.call-update) | async-done | bytes 65552 | tf_op jit(solution)/shard_map/psum | solution.py:92
  401.9 4.2 collective-permute-start.20
  407.5 5.7 collective-permute-start.22
  414.7 5.7 collective-permute-start.24
  421.9 5.7 collective-permute-start.26
  429.1 5.7 collective-permute-start.28
  436.4 5.7 collective-permute-start.30
  443.6 5.7 collective-permute-start.32
  450.8 7.2 %collective-permute-done.33 = f32[8,128]{1,0:T(8,128)S(1)} collective-permute-done((f32[8,128]{1,0:T(8,128)S(1)}, f32[8,128]{1,0:T(8,128)S(1)}, u32[]{:S(2)}, u32[]{:S(2)}) %collective-permute-start.33) | collective-permute-done | bytes 4128 | tf_op jit(solution)/shard_map/ppermute | solution.py:58
  461.5 4.6 all_to_all.79
  467.9 3.1 all_to_all.67
  471.0 2.4 broadcast_multiply_fusion
  473.4 2.5 copy.129
  475.9 2.2 scatter_fusion.2
  478.1 2.6 copy.130
  482.4 36.6 %psum.46 = f32[128]{0:T(128)S(1)} all-reduce(f32[128]{0:T(128)S(1)} %multiply_reduce_fusion), channel_id=1, replica_groups=mesh['sub'=16,'rhs'=2] {'sub'}, use_global_device_ids=true, to_apply=%region_14.15 | all-reduce | flops 128 | bytes 1024 | tf_op jit(solution)/shard_map/psum | solution.py:95
  518.9 2.2 fusion.32
  523.0 2.2 collective-permute-start.34
  541.4 2.3 subtract_multiply_fusion.3
  546.5 4.6 all_to_all.80
  552.9 3.1 all_to_all.71
  558.1 39.0 %psum.47 = f32[128]{0:T(128)S(1)} all-reduce(f32[128]{0:T(128)S(1)} %fusion.2), channel_id=1, replica_groups=mesh['sub'=16,'rhs'=2] {'sub'}, use_global_device_ids=true, to_apply=%region_16.17 | all-reduce | flops 128 | bytes 1024 | tf_op jit(solution)/shard_map/psum | solution.py:140
  597.1 2.5 multiply_add_fusion
  599.6 2.5 copy.143
  (207 shorter events, 101.8 us)
Async XLA Ops:
  7.4 191.7 %copy-start = (bf16[2,512,1024]{2,1,0:T(8,128)(2,1)S(1)}, bf16[2,512,1024]{2,1,0:T(8,128)(2,1)}, u32[]{:S(2)}) copy-start(bf16[2,512,1024]{2,1,0:T(8,128)(2,1)} %param.10) | copy-start | bytes 6291460
  16.6 16.1 %all-to-all-start = ((bf16[128,4,128]{2,1,0:T(4,128)(2,1)}), bf16[128,4,128]{2,1,0:T(4,128)(2,1)S(1)}, u32[]{:S(2)}, u32[]{:S(2)}) async-start(bf16[128,4,128]{2,1,0:T(4,128)(2,1)} %scatter_fusion), calls=%async_computation | async-start | bytes 262144 | tf_op jit(solution)/shard_map/all_to_all | solution.py:125
  24.9 114.9 %all-reduce.4.cloned.1.call-start = ((), (), s32[]{:S(2)}) async-start(), calls=%async_computation.6 | async-start | bytes 131072 | tf_op jit(solution)/shard_map/psum | solution.py:92
  35.9 165.1 %copy-start.1 = (f32[2,1024,128]{1,2,0:T(8,128)}, f32[2,1024,128]{1,2,0:T(8,128)S(1)}, u32[]{:S(2)}) copy-start(f32[2,1024,128]{1,2,0:T(8,128)S(1)} %get-tuple-element.34) | copy-start | bytes 3145732
  39.3 159.7 %all-gather.5.cloned.1.call-start = ((), (), s32[]{:S(2)}) async-start(), calls=%async_computation.5 | async-start | bytes 1572864 | tf_op jit(solution)/shard_map/all_gather | solution.py:22
  39.4 161.7 %copy-start.6 = (s32[1024]{0:T(1024)}, s32[1024]{0:T(1024)S(1)}, u32[]{:S(2)}) copy-start(s32[1024]{0:T(1024)S(1)} %pad_clamp_fusion) | copy-start | bytes 12292
  140.8 7.2 %collective-permute-start = (f32[8,128]{1,0:T(8,128)S(1)}, f32[8,128]{1,0:T(8,128)S(1)}, u32[]{:S(2)}, u32[]{:S(2)}) collective-permute-start(f32[8,128]{1,0:T(8,128)S(1)} %get-tuple-element.36), channel_id=1, source_target_pairs={{0,2},{2,4},{4,6},{6,8},{8,10},{10,12},{12,14},{14,16},{16,18},{18... | collective-permute-start | bytes 12296 | tf_op jit(solution)/shard_map/ppermute | solution.py:58
  142.3 5.8 collective-permute-start.1
  146.5 93.1 %all-gather.7.cloned.1.call-start = ((), (), s32[]{:S(2)}) async-start(), calls=%async_computation.7 | async-start | bytes 1572864 | tf_op jit(solution)/shard_map/all_gather | solution.py:22
  148.0 7.2 %collective-permute-start.2 = (f32[8,128]{1,0:T(8,128)S(1)}, f32[8,128]{1,0:T(8,128)S(1)}, u32[]{:S(2)}, u32[]{:S(2)}) collective-permute-start(f32[8,128]{1,0:T(8,128)S(1)} %collective-permute-done), channel_id=1, source_target_pairs={{0,2},{2,4},{4,6},{6,8},{8,10},{10,12},{12,14},{14,16},{16,18},{18... | collective-permute-start | bytes 12296 | tf_op jit(solution)/shard_map/ppermute | solution.py:58
  148.0 7.2 %collective-permute-start.3 = (f32[8,128]{1,0:T(8,128)S(1)}, f32[8,128]{1,0:T(8,128)S(1)}, u32[]{:S(2)}, u32[]{:S(2)}) collective-permute-start(f32[8,128]{1,0:T(8,128)S(1)} %collective-permute-done.1), channel_id=1, source_target_pairs={{0,30},{2,0},{4,2},{6,4},{8,6},{10,8},{12,10},{14,12},{16,14},{18,... | collective-permute-start | bytes 12296 | tf_op jit(solution)/shard_map/ppermute | solution.py:65
  155.2 7.2 %collective-permute-start.4 = (f32[8,128]{1,0:T(8,128)S(1)}, f32[8,128]{1,0:T(8,128)S(1)}, u32[]{:S(2)}, u32[]{:S(2)}) collective-permute-start(f32[8,128]{1,0:T(8,128)S(1)} %collective-permute-done.2), channel_id=1, source_target_pairs={{0,2},{2,4},{4,6},{6,8},{8,10},{10,12},{12,14},{14,16},{16,18},{18... | collective-permute-start | bytes 12296 | tf_op jit(solution)/shard_map/ppermute | solution.py:58
  155.2 7.2 %collective-permute-start.5 = (f32[8,128]{1,0:T(8,128)S(1)}, f32[8,128]{1,0:T(8,128)S(1)}, u32[]{:S(2)}, u32[]{:S(2)}) collective-permute-start(f32[8,128]{1,0:T(8,128)S(1)} %collective-permute-done.3), channel_id=1, source_target_pairs={{0,30},{2,0},{4,2},{6,4},{8,6},{10,8},{12,10},{14,12},{16,14},{18,... | collective-permute-start | bytes 12296 | tf_op jit(solution)/shard_map/ppermute | solution.py:65
  162.4 7.2 %collective-permute-start.6 = (f32[8,128]{1,0:T(8,128)S(1)}, f32[8,128]{1,0:T(8,128)S(1)}, u32[]{:S(2)}, u32[]{:S(2)}) collective-permute-start(f32[8,128]{1,0:T(8,128)S(1)} %collective-permute-done.4), channel_id=1, source_target_pairs={{0,2},{2,4},{4,6},{6,8},{8,10},{10,12},{12,14},{14,16},{16,18},{18... | collective-permute-start | bytes 12296 | tf_op jit(solution)/shard_map/ppermute | solution.py:58
  162.4 7.2 %collective-permute-start.7 = (f32[8,128]{1,0:T(8,128)S(1)}, f32[8,128]{1,0:T(8,128)S(1)}, u32[]{:S(2)}, u32[]{:S(2)}) collective-permute-start(f32[8,128]{1,0:T(8,128)S(1)} %collective-permute-done.5), channel_id=1, source_target_pairs={{0,30},{2,0},{4,2},{6,4},{8,6},{10,8},{12,10},{14,12},{16,14},{18,... | collective-permute-start | bytes 12296 | tf_op jit(solution)/shard_map/ppermute | solution.py:65
  169.6 7.2 %collective-permute-start.8 = (f32[8,128]{1,0:T(8,128)S(1)}, f32[8,128]{1,0:T(8,128)S(1)}, u32[]{:S(2)}, u32[]{:S(2)}) collective-permute-start(f32[8,128]{1,0:T(8,128)S(1)} %collective-permute-done.6), channel_id=1, source_target_pairs={{0,2},{2,4},{4,6},{6,8},{8,10},{10,12},{12,14},{14,16},{16,18},{18... | collective-permute-start | bytes 12296 | tf_op jit(solution)/shard_map/ppermute | solution.py:58
  169.6 7.2 %collective-permute-start.9 = (f32[8,128]{1,0:T(8,128)S(1)}, f32[8,128]{1,0:T(8,128)S(1)}, u32[]{:S(2)}, u32[]{:S(2)}) collective-permute-start(f32[8,128]{1,0:T(8,128)S(1)} %collective-permute-done.7), channel_id=1, source_target_pairs={{0,30},{2,0},{4,2},{6,4},{8,6},{10,8},{12,10},{14,12},{16,14},{18,... | collective-permute-start | bytes 12296 | tf_op jit(solution)/shard_map/ppermute | solution.py:65
  176.8 7.2 %collective-permute-start.10 = (f32[8,128]{1,0:T(8,128)S(1)}, f32[8,128]{1,0:T(8,128)S(1)}, u32[]{:S(2)}, u32[]{:S(2)}) collective-permute-start(f32[8,128]{1,0:T(8,128)S(1)} %collective-permute-done.8), channel_id=1, source_target_pairs={{0,2},{2,4},{4,6},{6,8},{8,10},{10,12},{12,14},{14,16},{16,18},{18... | collective-permute-start | bytes 12296 | tf_op jit(solution)/shard_map/ppermute | solution.py:58
  176.8 7.2 %collective-permute-start.11 = (f32[8,128]{1,0:T(8,128)S(1)}, f32[8,128]{1,0:T(8,128)S(1)}, u32[]{:S(2)}, u32[]{:S(2)}) collective-permute-start(f32[8,128]{1,0:T(8,128)S(1)} %collective-permute-done.9), channel_id=1, source_target_pairs={{0,30},{2,0},{4,2},{6,4},{8,6},{10,8},{12,10},{14,12},{16,14},{18,... | collective-permute-start | bytes 12296 | tf_op jit(solution)/shard_map/ppermute | solution.py:65
  184.0 7.2 %collective-permute-start.12 = (f32[8,128]{1,0:T(8,128)S(1)}, f32[8,128]{1,0:T(8,128)S(1)}, u32[]{:S(2)}, u32[]{:S(2)}) collective-permute-start(f32[8,128]{1,0:T(8,128)S(1)} %collective-permute-done.10), channel_id=1, source_target_pairs={{0,2},{2,4},{4,6},{6,8},{8,10},{10,12},{12,14},{14,16},{16,18},{18... | collective-permute-start | bytes 12296 | tf_op jit(solution)/shard_map/ppermute | solution.py:58
  184.0 7.2 %collective-permute-start.13 = (f32[8,128]{1,0:T(8,128)S(1)}, f32[8,128]{1,0:T(8,128)S(1)}, u32[]{:S(2)}, u32[]{:S(2)}) collective-permute-start(f32[8,128]{1,0:T(8,128)S(1)} %collective-permute-done.11), channel_id=1, source_target_pairs={{0,30},{2,0},{4,2},{6,4},{8,6},{10,8},{12,10},{14,12},{16,14},{18,... | collective-permute-start | bytes 12296 | tf_op jit(solution)/shard_map/ppermute | solution.py:65
  191.2 7.2 %collective-permute-start.14 = (f32[8,128]{1,0:T(8,128)S(1)}, f32[8,128]{1,0:T(8,128)S(1)}, u32[]{:S(2)}, u32[]{:S(2)}) collective-permute-start(f32[8,128]{1,0:T(8,128)S(1)} %collective-permute-done.12), channel_id=1, source_target_pairs={{0,2},{2,4},{4,6},{6,8},{8,10},{10,12},{12,14},{14,16},{16,18},{18... | collective-permute-start | bytes 12296 | tf_op jit(solution)/shard_map/ppermute | solution.py:58
  218.3 5.5 collective-permute-start.15
  219.2 180.1 %all-reduce.6.cloned.1.call-start = ((), (), s32[]{:S(2)}) async-start(), calls=%async_computation.9 | async-start | bytes 131072 | tf_op jit(solution)/shard_map/psum | solution.py:92
  219.4 7.4 %collective-permute-start.16 = (bf16[2,256,128]{1,2,0:T(8,128)(2,1)}, bf16[2,256,128]{1,2,0:T(8,128)(2,1)}, u32[]{:S(2)}, u32[]{:S(2)}) collective-permute-start(bf16[2,256,128]{1,2,0:T(8,128)(2,1)} %get-tuple-element.30), channel_id=1, source_target_pairs={{0,4},{2,6},{4,0},{6,2},{8,12},{10,14},{12,8},{14,10},{16,20},{18,... | collective-permute-start | bytes 393224 | tf_op jit(solution)/shard_map/ppermute | solution.py:15
  219.5 11.1 %collective-permute-start.17 = (bf16[2,256,128]{1,2,0:T(8,128)(2,1)}, bf16[2,256,128]{1,2,0:T(8,128)(2,1)}, u32[]{:S(2)}, u32[]{:S(2)}) collective-permute-start(bf16[2,256,128]{1,2,0:T(8,128)(2,1)} %get-tuple-element.29), channel_id=1, source_target_pairs={{0,8},{2,10},{4,12},{6,14},{8,0},{10,2},{12,4},{14,6},{16,24},{18,... | collective-permute-start | bytes 393224 | tf_op jit(solution)/shard_map/ppermute | solution.py:15
  219.6 14.8 %collective-permute-start.18 = (bf16[2,256,128]{1,2,0:T(8,128)(2,1)}, bf16[2,256,128]{1,2,0:T(8,128)(2,1)S(1)}, u32[]{:S(2)}, u32[]{:S(2)}) collective-permute-start(bf16[2,256,128]{1,2,0:T(8,128)(2,1)} %get-tuple-element.28), channel_id=1, source_target_pairs={{0,16},{2,18},{4,20},{6,22},{8,24},{10,26},{12,28},{14,30},{16,0},... | collective-permute-start | bytes 393224 | tf_op jit(solution)/shard_map/ppermute | solution.py:15
  301.3 157.3 %all-gather.9.cloned.1.call-start = ((), (), s32[]{:S(2)}) async-start(), calls=%async_computation.8 | async-start | bytes 1572864 | tf_op jit(solution)/shard_map/all_gather | solution.py:22
  400.3 7.2 %collective-permute-start.19 = (f32[8,128]{1,0:T(8,128)S(1)}, f32[8,128]{1,0:T(8,128)S(1)}, u32[]{:S(2)}, u32[]{:S(2)}) collective-permute-start(f32[8,128]{1,0:T(8,128)S(1)} %get-tuple-element.38), channel_id=1, source_target_pairs={{0,2},{2,4},{4,6},{6,8},{8,10},{10,12},{12,14},{14,16},{16,18},{18... | collective-permute-start | bytes 12296 | tf_op jit(solution)/shard_map/ppermute | solution.py:58
  401.8 141.9 %all-gather.11.cloned.1.call-start = ((), (), s32[]{:S(2)}) async-start(), calls=%async_computation.10 | async-start | bytes 1572864 | tf_op jit(solution)/shard_map/all_gather | solution.py:22
  401.9 5.7 collective-permute-start.20
  407.5 7.2 %collective-permute-start.21 = (f32[8,128]{1,0:T(8,128)S(1)}, f32[8,128]{1,0:T(8,128)S(1)}, u32[]{:S(2)}, u32[]{:S(2)}) collective-permute-start(f32[8,128]{1,0:T(8,128)S(1)} %collective-permute-done.19), channel_id=1, source_target_pairs={{0,2},{2,4},{4,6},{6,8},{8,10},{10,12},{12,14},{14,16},{16,18},{18... | collective-permute-start | bytes 12296 | tf_op jit(solution)/shard_map/ppermute | solution.py:58
  407.5 7.2 %collective-permute-start.22 = (f32[8,128]{1,0:T(8,128)S(1)}, f32[8,128]{1,0:T(8,128)S(1)}, u32[]{:S(2)}, u32[]{:S(2)}) collective-permute-start(f32[8,128]{1,0:T(8,128)S(1)} %collective-permute-done.20), channel_id=1, source_target_pairs={{0,30},{2,0},{4,2},{6,4},{8,6},{10,8},{12,10},{14,12},{16,14},{18,... | collective-permute-start | bytes 12296 | tf_op jit(solution)/shard_map/ppermute | solution.py:65
  414.7 7.2 %collective-permute-start.23 = (f32[8,128]{1,0:T(8,128)S(1)}, f32[8,128]{1,0:T(8,128)S(1)}, u32[]{:S(2)}, u32[]{:S(2)}) collective-permute-start(f32[8,128]{1,0:T(8,128)S(1)} %collective-permute-done.21), channel_id=1, source_target_pairs={{0,2},{2,4},{4,6},{6,8},{8,10},{10,12},{12,14},{14,16},{16,18},{18... | collective-permute-start | bytes 12296 | tf_op jit(solution)/shard_map/ppermute | solution.py:58
  414.7 7.2 %collective-permute-start.24 = (f32[8,128]{1,0:T(8,128)S(1)}, f32[8,128]{1,0:T(8,128)S(1)}, u32[]{:S(2)}, u32[]{:S(2)}) collective-permute-start(f32[8,128]{1,0:T(8,128)S(1)} %collective-permute-done.22), channel_id=1, source_target_pairs={{0,30},{2,0},{4,2},{6,4},{8,6},{10,8},{12,10},{14,12},{16,14},{18,... | collective-permute-start | bytes 12296 | tf_op jit(solution)/shard_map/ppermute | solution.py:65
  421.9 7.2 %collective-permute-start.25 = (f32[8,128]{1,0:T(8,128)S(1)}, f32[8,128]{1,0:T(8,128)S(1)}, u32[]{:S(2)}, u32[]{:S(2)}) collective-permute-start(f32[8,128]{1,0:T(8,128)S(1)} %collective-permute-done.23), channel_id=1, source_target_pairs={{0,2},{2,4},{4,6},{6,8},{8,10},{10,12},{12,14},{14,16},{16,18},{18... | collective-permute-start | bytes 12296 | tf_op jit(solution)/shard_map/ppermute | solution.py:58
  421.9 7.2 %collective-permute-start.26 = (f32[8,128]{1,0:T(8,128)S(1)}, f32[8,128]{1,0:T(8,128)S(1)}, u32[]{:S(2)}, u32[]{:S(2)}) collective-permute-start(f32[8,128]{1,0:T(8,128)S(1)} %collective-permute-done.24), channel_id=1, source_target_pairs={{0,30},{2,0},{4,2},{6,4},{8,6},{10,8},{12,10},{14,12},{16,14},{18,... | collective-permute-start | bytes 12296 | tf_op jit(solution)/shard_map/ppermute | solution.py:65
  429.1 7.2 %collective-permute-start.27 = (f32[8,128]{1,0:T(8,128)S(1)}, f32[8,128]{1,0:T(8,128)S(1)}, u32[]{:S(2)}, u32[]{:S(2)}) collective-permute-start(f32[8,128]{1,0:T(8,128)S(1)} %collective-permute-done.25), channel_id=1, source_target_pairs={{0,2},{2,4},{4,6},{6,8},{8,10},{10,12},{12,14},{14,16},{16,18},{18... | collective-permute-start | bytes 12296 | tf_op jit(solution)/shard_map/ppermute | solution.py:58
  429.1 7.2 %collective-permute-start.28 = (f32[8,128]{1,0:T(8,128)S(1)}, f32[8,128]{1,0:T(8,128)S(1)}, u32[]{:S(2)}, u32[]{:S(2)}) collective-permute-start(f32[8,128]{1,0:T(8,128)S(1)} %collective-permute-done.26), channel_id=1, source_target_pairs={{0,30},{2,0},{4,2},{6,4},{8,6},{10,8},{12,10},{14,12},{16,14},{18,... | collective-permute-start | bytes 12296 | tf_op jit(solution)/shard_map/ppermute | solution.py:65
  436.3 7.2 %collective-permute-start.29 = (f32[8,128]{1,0:T(8,128)S(1)}, f32[8,128]{1,0:T(8,128)S(1)}, u32[]{:S(2)}, u32[]{:S(2)}) collective-permute-start(f32[8,128]{1,0:T(8,128)S(1)} %collective-permute-done.27), channel_id=1, source_target_pairs={{0,2},{2,4},{4,6},{6,8},{8,10},{10,12},{12,14},{14,16},{16,18},{18... | collective-permute-start | bytes 12296 | tf_op jit(solution)/shard_map/ppermute | solution.py:58
  436.4 7.2 %collective-permute-start.30 = (f32[8,128]{1,0:T(8,128)S(1)}, f32[8,128]{1,0:T(8,128)S(1)}, u32[]{:S(2)}, u32[]{:S(2)}) collective-permute-start(f32[8,128]{1,0:T(8,128)S(1)} %collective-permute-done.28), channel_id=1, source_target_pairs={{0,30},{2,0},{4,2},{6,4},{8,6},{10,8},{12,10},{14,12},{16,14},{18,... | collective-permute-start | bytes 12296 | tf_op jit(solution)/shard_map/ppermute | solution.py:65
  443.6 7.2 %collective-permute-start.31 = (f32[8,128]{1,0:T(8,128)S(1)}, f32[8,128]{1,0:T(8,128)S(1)}, u32[]{:S(2)}, u32[]{:S(2)}) collective-permute-start(f32[8,128]{1,0:T(8,128)S(1)} %collective-permute-done.29), channel_id=1, source_target_pairs={{0,2},{2,4},{4,6},{6,8},{8,10},{10,12},{12,14},{14,16},{16,18},{18... | collective-permute-start | bytes 12296 | tf_op jit(solution)/shard_map/ppermute | solution.py:58
  443.6 7.2 %collective-permute-start.32 = (f32[8,128]{1,0:T(8,128)S(1)}, f32[8,128]{1,0:T(8,128)S(1)}, u32[]{:S(2)}, u32[]{:S(2)}) collective-permute-start(f32[8,128]{1,0:T(8,128)S(1)} %collective-permute-done.30), channel_id=1, source_target_pairs={{0,30},{2,0},{4,2},{6,4},{8,6},{10,8},{12,10},{14,12},{16,14},{18,... | collective-permute-start | bytes 12296 | tf_op jit(solution)/shard_map/ppermute | solution.py:65
  450.8 7.2 %collective-permute-start.33 = (f32[8,128]{1,0:T(8,128)S(1)}, f32[8,128]{1,0:T(8,128)S(1)}, u32[]{:S(2)}, u32[]{:S(2)}) collective-permute-start(f32[8,128]{1,0:T(8,128)S(1)} %collective-permute-done.31), channel_id=1, source_target_pairs={{0,2},{2,4},{4,6},{6,8},{8,10},{10,12},{12,14},{14,16},{16,18},{18... | collective-permute-start | bytes 12296 | tf_op jit(solution)/shard_map/ppermute | solution.py:58
  523.0 5.1 collective-permute-start.34
  525.2 5.8 collective-permute-start.35
  525.2 9.5 %collective-permute-start.36 = (bf16[2,256,128]{1,2,0:T(8,128)(2,1)}, bf16[2,256,128]{1,2,0:T(8,128)(2,1)}, u32[]{:S(2)}, u32[]{:S(2)}) collective-permute-start(bf16[2,256,128]{1,2,0:T(8,128)(2,1)} %get-tuple-element.21), channel_id=1, source_target_pairs={{0,8},{2,10},{4,12},{6,14},{8,0},{10,2},{12,4},{14,6},{16,24},{18,... | collective-permute-start | bytes 393224 | tf_op jit(solution)/shard_map/ppermute | solution.py:15
  525.3 13.2 %collective-permute-start.37 = (bf16[2,256,128]{1,2,0:T(8,128)(2,1)}, bf16[2,256,128]{1,2,0:T(8,128)(2,1)S(1)}, u32[]{:S(2)}, u32[]{:S(2)}) collective-permute-start(bf16[2,256,128]{1,2,0:T(8,128)(2,1)} %get-tuple-element.20), channel_id=1, source_target_pairs={{0,16},{2,18},{4,20},{6,22},{8,24},{10,26},{12,28},{14,30},{16,0},... | collective-permute-start | bytes 393224 | tf_op jit(solution)/shard_map/ppermute | solution.py:15
  (13 other events, 309.6 us)
Sparse Core Ops, SparseCore 0:
  39.4 100.3 all-reduce.3
  301.5 97.8 all-reduce.5
Sparse Core Ops, SparseCore 1:
  146.6 5.2 all-gather.4
  219.3 6.7 all-gather.6
  401.9 8.8 all-gather.8
  525.2 5.1 all-gather.10
